TPU v7x, 512 devices: a whole 4x4x16 slice. The times are simulated.
512 devices in a mesh: cell: 64 (over z, y_lo, core), inst: 8 (over x, y_hi).
Axes of the slice: x: 4, y: 4 (y_hi: 2, y_lo: 2; y = y_hi * 2 + y_lo), z: 16, core: 2. Of those that a mesh axis runs over, the one named last changes fastest.
Arguments:
- initial: float32 [80, 131072], P('inst', 'cell'), may hold values from -6 to 6
- source: float32 [80, 131072], P('inst', 'cell'), may hold values from -6 to 6
- neighbors: int32 [4, 131072], P(None, 'cell'), may hold values from -256 to 256, as said below
- face_weights: float32 [4, 131072], P(None, 'cell'), may hold values from 0.25 to 1
- damping: float32 [131072], P('cell'), may hold values from 0.5 to 2
Outputs:
- solution: float32 [80, 131072], P('inst', 'cell')
Inputs may be any that keep to these rules, and one draw needn't show every extreme that they name: `neighbors`: entries 0 and 2 of a cell's offsets are at or below zero, entries 1 and 3 at or above zero; a cell plus each of its offsets is a cell of the grid; in every draw some offsets are exactly -256 and exactly 256.
All inputs are finite; a program needn't handle non-finite values.
Results may differ from a plain program's by a relative error of at most 0.0001.
Values sent between devices are 32-bit elements; how exact they have to be, the bound alone decides.
A program may use at most 64 MiB of HBM per device.

v0:
```python
import jax
import jax.numpy as jnp
from jax import lax
from jax.sharding import PartitionSpec as P

NI = 16
NC = 4
COMP = 5
NEIGH = 4
SWEEPS_FINE = 2
SWEEPS_COARSE = 3
PLANE = 256
FREQ = 0.15
RELAX = 0.6


def padded_2(block, sides, width):
    for axis, dim in sides:
        count = lax.axis_size(axis)
        forward = [(i, i + 1) for i in range(count - 1)]
        backward = [(target, source) for source, target in forward]
        low = lax.ppermute(
            lax.slice_in_dim(block, block.shape[dim] - width, None, axis=dim), axis, forward
        )
        high = lax.ppermute(lax.slice_in_dim(block, 0, width, axis=dim), axis, backward)
        block = jnp.concatenate([low, block, high], axis=dim)
    return block


def spectral_matrix(points):
    steps = jnp.arange(points, dtype=jnp.float32)
    offset = steps[:, None] - steps[None, :]
    parity = 1.0 - 2.0 * jnp.mod(offset, 2.0)
    angle = jnp.where(offset == 0, 0.5, jnp.pi * offset / points)
    return jnp.where(offset == 0, 0.0, 0.5 * parity / jnp.tan(angle))


def restrict_matrix():
    coarse_t = jnp.arange(NC, dtype=jnp.float32) / NC
    fine_t = jnp.arange(NI, dtype=jnp.float32) / NI
    return (1.0 + 2.0 * jnp.cos(2.0 * jnp.pi * (coarse_t[:, None] - fine_t[None, :]))) / NI


def prolong_matrix():
    coarse_t = jnp.arange(NC, dtype=jnp.float32) / NC
    fine_t = jnp.arange(NI, dtype=jnp.float32) / NI
    return (1.0 + 2.0 * jnp.cos(2.0 * jnp.pi * (fine_t[:, None] - coarse_t[None, :]))) / NC


def expand(matrix):
    return jnp.kron(matrix, jnp.eye(COMP, dtype=jnp.float32))


def neighbour_terms(padded, flat_index, face_weights):
    cells = face_weights.shape[1]
    picked = jnp.take(padded, flat_index, axis=1).reshape(padded.shape[0], NEIGH, cells)
    return jnp.sum(face_weights[None, :, :] * picked, axis=1)


def fine_stencil(values, flat_index, face_weights):
    padded = padded_2(values, (("cell", 1),), PLANE)
    return neighbour_terms(padded, flat_index, face_weights)


def coarse_stencil(values, flat_index, face_weights):
    padded = padded_2(values, ((("cell", "inst"), 1),), PLANE)
    return neighbour_terms(padded, flat_index, face_weights)


def per_device(initial, source, neighbors, face_weights, damping):
    cells = initial.shape[1]
    own_count = initial.shape[0]
    inst_count = lax.axis_size("inst")
    inst_id = lax.axis_index("inst")
    highest = lax.Precision.HIGHEST
    fine_matrix = expand(spectral_matrix(NI))
    coarse_matrix = expand(spectral_matrix(NC))
    own_rows = lax.dynamic_slice_in_dim(fine_matrix, inst_id * own_count, own_count, 0)
    diagonal = damping + jnp.sum(face_weights, axis=0)
    position = jnp.arange(cells, dtype=jnp.int32)
    fine_index = (neighbors + position[None, :] + PLANE).reshape(-1)

    def derivative(values):
        gathered = lax.all_gather(values, "inst", axis=0, tiled=True)
        return jnp.dot(own_rows, gathered, precision=highest)

    def fine_operator(values):
        return (
            FREQ * derivative(values)
            + diagonal * values
            - fine_stencil(values, fine_index, face_weights)
        )

    solution = initial
    for sweep in range(SWEEPS_FINE):
        solution = solution + RELAX * (source - fine_operator(solution)) / diagonal
    residual = source - fine_operator(solution)
    own_columns = lax.dynamic_slice_in_dim(
        expand(restrict_matrix()), inst_id * own_count, own_count, 1
    )
    partial_terms = jnp.dot(own_columns, residual, precision=highest)
    prolong_rows = lax.dynamic_slice_in_dim(
        expand(prolong_matrix()), inst_id * own_count, own_count, 0
    )
    coarse_rhs = lax.psum_scatter(partial_terms, "inst", scatter_dimension=1, tiled=True)
    share = cells // inst_count
    share_weights = lax.dynamic_slice_in_dim(face_weights, inst_id * share, share, 1)
    share_diagonal = lax.dynamic_slice_in_dim(diagonal, inst_id * share, share, 0)
    share_offsets = lax.dynamic_slice_in_dim(neighbors, inst_id * share, share, 1)
    share_position = jnp.arange(share, dtype=jnp.int32)
    share_index = (share_offsets + share_position[None, :] + PLANE).reshape(-1)
    correction = RELAX * coarse_rhs / share_diagonal
    for sweep in range(SWEEPS_COARSE - 1):
        spectral = jnp.dot(coarse_matrix, correction, precision=highest)
        applied = (
            FREQ * spectral
            + share_diagonal * correction
            - coarse_stencil(correction, share_index, share_weights)
        )
        correction = correction + RELAX * (coarse_rhs - applied) / share_diagonal
    whole_correction = lax.all_gather(correction, "inst", axis=1, tiled=True)
    return solution + jnp.dot(prolong_rows, whole_correction, precision=highest)


def solution(mesh):
    return jax.shard_map(
        per_device,
        mesh=mesh,
        in_specs=(
            P("inst", "cell"),
            P("inst", "cell"),
            P(None, "cell"),
            P(None, "cell"),
            P("cell"),
        ),
        out_specs=P("inst", "cell"),
        check_vma=False,
    )
```

profile of v0, /device:TPU:128, one launch (start us, length us, event | category | flops | bytes accessed | tf_op | source)
XLA Modules:
  0.0 418.6 jit_solution(3546796274003178314)
XLA Ops:
  6.5 0.8 fusion.63
  7.3 1.9 collective-permute-start
  9.2 5.8 %collective-permute-start.1 = (f32[10,256]{1,0:T(8,128)S(1)}, f32[10,256]{1,0:T(8,128)S(1)}, u32[]{:S(2)}, u32[]{:S(2)}) collective-permute-start(f32[10,256]{1,0:T(8,128)S(1)} %get-tuple-element.12), channel_id=1, source_target_pairs={{8,0},{16,8},{24,16},{32,24},{40,32},{48,40},{56,48},{64,56},{72,6... | collective-permute-start | bytes 30728 | tf_op jit(solution)/shard_map/ppermute | solution.py:25
  15.0 0.8 add_bitcast_fusion
  16.0 0.7 add_bitcast_fusion.1
  16.7 38.0 %all-gather = f32[8,10,2048]{2,1,0:T(8,128)S(1)} all-gather(f32[1,10,2048]{2,1,0:T(8,128)} %bitcast.47), channel_id=1, replica_groups=mesh['cell'=64,'inst'=8] {'inst'}, dimensions={0}, use_global_device_ids=true | all-gather | bytes 737280 | tf_op jit(solution)/shard_map/all_gather | solution.py:84
  55.1 0.3 mul.297
  55.8 0.4 copy.21
  56.2 27.8 %gather_fusion = f32[8192,10]{1,0:T(8,128)} fusion(f32[10,2560]{0,1:T(8,128)S(1)} %copy.21, s32[8192]{0:T(1024)S(1)} %fusion.27), kind=kCustom, calls=%fused_computation.clone | custom fusion | bytes 688128 | tf_op jit(solution)/shard_map/jit(_take)/gather | solution.py:56
  84.1 6.2 %broadcast_select_fusion.2 = f32[8192,10]{1,0:T(8,128)S(1)} fusion(f32[8192,10]{1,0:T(8,128)} %gather_fusion, pred[8192]{0:T(1024)(128)(4,1)S(1)} %compare_and_fusion), kind=kLoop, calls=%fused_computation.29 | loop fusion | flops 81920 | bytes 663552 | tf_op jit(solution)/shard_map/jit(_take)/select_n | solution.py:56
  90.3 1.6 multiply_reduce_fusion.2
  91.9 0.3 copy.22
  92.2 0.5 fusion.14
  92.7 1.9 collective-permute-start.2
  94.6 5.8 %collective-permute-start.3 = (f32[10,256]{1,0:T(8,128)S(1)}, f32[10,256]{1,0:T(8,128)S(1)}, u32[]{:S(2)}, u32[]{:S(2)}) collective-permute-start(f32[10,256]{1,0:T(8,128)S(1)} %get-tuple-element.10), channel_id=1, source_target_pairs={{8,0},{16,8},{24,16},{32,24},{40,32},{48,40},{56,48},{64,56},{72,6... | collective-permute-start | bytes 30728 | tf_op jit(solution)/shard_map/ppermute | solution.py:25
  100.4 36.9 %all-gather.1 = f32[8,10,2048]{2,1,0:T(8,128)S(1)} all-gather(f32[1,10,2048]{2,1,0:T(8,128)S(1)} %bitcast.44), channel_id=1, replica_groups=mesh['cell'=64,'inst'=8] {'inst'}, dimensions={0}, use_global_device_ids=true | all-gather | bytes 737280 | tf_op jit(solution)/shard_map/all_gather | solution.py:84
  137.5 0.4 copy.23
  137.9 27.8 %gather_fusion.1 = f32[8192,10]{1,0:T(8,128)} fusion(f32[10,2560]{0,1:T(8,128)S(1)} %copy.23, s32[8192]{0:T(1024)S(1)} %fusion.27), kind=kCustom, calls=%fused_computation.2.clone | custom fusion | bytes 688128 | tf_op jit(solution)/shard_map/jit(_take)/gather | solution.py:56
  165.8 6.2 %broadcast_select_fusion.1 = f32[8192,10]{1,0:T(8,128)S(1)} fusion(f32[8192,10]{1,0:T(8,128)} %gather_fusion.1, pred[8192]{0:T(1024)(128)(4,1)S(1)} %compare_and_fusion), kind=kLoop, calls=%fused_computation.28 | loop fusion | flops 81920 | bytes 663552 | tf_op jit(solution)/shard_map/jit(_take)/select_n | solution.py:56
  172.0 1.6 multiply_reduce_fusion.1
  173.6 0.3 copy.24
  173.9 0.4 fusion.8
  174.4 1.9 collective-permute-start.4
  176.3 5.8 %collective-permute-start.5 = (f32[10,256]{1,0:T(8,128)S(1)}, f32[10,256]{1,0:T(8,128)S(1)}, u32[]{:S(2)}, u32[]{:S(2)}) collective-permute-start(f32[10,256]{1,0:T(8,128)S(1)} %get-tuple-element.8), channel_id=1, source_target_pairs={{8,0},{16,8},{24,16},{32,24},{40,32},{48,40},{56,48},{64,56},{72,6... | collective-permute-start | bytes 30728 | tf_op jit(solution)/shard_map/ppermute | solution.py:25
  182.1 36.5 %all-gather.2 = f32[8,10,2048]{2,1,0:T(8,128)S(1)} all-gather(f32[1,10,2048]{2,1,0:T(8,128)S(1)} %bitcast.43), channel_id=1, replica_groups=mesh['cell'=64,'inst'=8] {'inst'}, dimensions={0}, use_global_device_ids=true | all-gather | bytes 737280 | tf_op jit(solution)/shard_map/all_gather | solution.py:84
  218.7 0.4 copy.26
  219.1 27.8 %gather_fusion.2 = f32[8192,10]{1,0:T(8,128)} fusion(f32[10,2560]{0,1:T(8,128)S(1)} %copy.26, s32[8192]{0:T(1024)S(1)} %fusion.27), kind=kCustom, calls=%fused_computation.3.clone | custom fusion | bytes 688128 | tf_op jit(solution)/shard_map/jit(_take)/gather | solution.py:56
  247.0 6.2 %broadcast_select_fusion = f32[8192,10]{1,0:T(8,128)S(1)} fusion(f32[8192,10]{1,0:T(8,128)} %gather_fusion.2, pred[8192]{0:T(1024)(128)(4,1)S(1)} %compare_and_fusion), kind=kLoop, calls=%fused_computation.27 | loop fusion | flops 81920 | bytes 663552 | tf_op jit(solution)/shard_map/jit(_take)/select_n | solution.py:56
  253.2 1.6 multiply_reduce_fusion
  254.8 0.3 copy.27
  255.1 0.4 fusion.2
  255.5 1.0 fusion.28
  256.7 85.6 %reduce-scatter.2.cloned.1.call-done = f32[20,256]{1,0:T(8,128)} async-done(((f32[20,2048]{1,0:T(8,128)}), f32[20,256]{1,0:T(8,128)}) %reduce-scatter.2.cloned.1.call-update) | async-done | bytes 20496 | tf_op jit(solution)/shard_map/reduce_scatter | solution.py:105
  342.4 0.8 multiply_divide_fusion
  343.2 4.3 %collective-permute-start.6 = (f32[20,256]{1,0:T(8,128)S(1)}, f32[20,256]{1,0:T(8,128)S(1)}, u32[]{:S(2)}, u32[]{:S(2)}) collective-permute-start(f32[20,256]{1,0:T(8,128)S(1)} %multiply_divide_fusion), channel_id=1, source_target_pairs={{0,1},{1,2},{2,3},{3,4},{4,5},{5,6},{6,7},{7,8},{8,9},{9,10},{10,1... | collective-permute-start | bytes 61448 | tf_op jit(solution)/shard_map/ppermute | solution.py:22
  347.5 6.7 %collective-permute-start.7 = (f32[20,256]{1,0:T(8,128)S(1)}, f32[20,256]{1,0:T(8,128)S(1)}, u32[]{:S(2)}, u32[]{:S(2)}) collective-permute-start(f32[20,256]{1,0:T(8,128)S(1)} %multiply_divide_fusion), channel_id=1, source_target_pairs={{1,0},{2,1},{3,2},{4,3},{5,4},{6,5},{7,6},{8,7},{9,8},{10,9},{11,1... | collective-permute-start | bytes 61448 | tf_op jit(solution)/shard_map/ppermute | solution.py:25
  354.4 1.3 collective-permute-done.7
  355.9 2.8 gather_fusion.3
  358.9 0.2 multiply_reduce_fusion.4
  359.2 1.0 fusion.26
  360.2 3.6 collective-permute-start.8
  363.7 7.4 %collective-permute-start.9 = (f32[20,256]{1,0:T(8,128)S(1)}, f32[20,256]{1,0:T(8,128)S(1)}, u32[]{:S(2)}, u32[]{:S(2)}) collective-permute-start(f32[20,256]{1,0:T(8,128)S(1)} %fusion.26), channel_id=1, source_target_pairs={{1,0},{2,1},{3,2},{4,3},{5,4},{6,5},{7,6},{8,7},{9,8},{10,9},{11,1... | collective-permute-start | bytes 61448 | tf_op jit(solution)/shard_map/ppermute | solution.py:25
  371.4 1.3 collective-permute-done.9
  372.9 2.8 gather_fusion.4
  375.7 0.2 broadcast_select_fusion.3
  375.9 0.2 multiply_reduce_fusion.3
  376.4 34.3 %all_gather.15 = f32[20,2048]{1,0:T(8,128)S(1)} all-gather(f32[20,256]{1,0:T(8,128)S(1)} %fusion.20), channel_id=1, replica_groups=mesh['cell'=64,'inst'=8] {'inst'}, dimensions={1}, use_global_device_ids=true | all-gather | bytes 184320 | tf_op jit(solution)/shard_map/all_gather | solution.py:121
  410.7 1.1 convolution_add_fusion
  (61 shorter events, 2.6 us)
Async XLA Ops:
  6.5 49.2 %copy-start = (f32[10,2048]{1,0:T(8,128)S(1)}, f32[10,2048]{1,0:T(8,128)}, u32[]{:S(2)}) copy-start(f32[10,2048]{1,0:T(8,128)} %param.9) | copy-start | bytes 245764
  6.5 49.1 %copy-start.2 = (f32[4,2048]{1,0:T(4,128)S(1)}, f32[4,2048]{1,0:T(4,128)}, u32[]{:S(2)}) copy-start(f32[4,2048]{1,0:T(4,128)} %param.12) | copy-start | bytes 98308
  6.5 49.1 %copy-start.4 = (f32[2048]{0:T(1024)S(1)}, f32[2048]{0:T(1024)}, u32[]{:S(2)}) copy-start(f32[2048]{0:T(1024)} %param.13) | copy-start | bytes 24580
  6.5 335.8 %reduce-scatter.2.cloned.1.call-start = ((), (), s32[]{:S(2)}) async-start(), calls=%async_computation.1 | async-start | bytes 221184 | tf_op jit(solution)/shard_map/reduce_scatter | solution.py:105
  7.3 48.4 %collective-permute-start = (f32[10,256]{1,0:T(8,128)S(1)}, f32[10,256]{1,0:T(8,128)S(1)}, u32[]{:S(2)}, u32[]{:S(2)}) collective-permute-start(f32[10,256]{1,0:T(8,128)S(1)} %get-tuple-element.11), channel_id=1, source_target_pairs={{0,8},{8,16},{16,24},{24,32},{32,40},{40,48},{48,56},{56,64},{64,7... | collective-permute-start | bytes 30728 | tf_op jit(solution)/shard_map/ppermute | solution.py:22
  9.2 46.5 %collective-permute-start.1 = (f32[10,256]{1,0:T(8,128)S(1)}, f32[10,256]{1,0:T(8,128)S(1)}, u32[]{:S(2)}, u32[]{:S(2)}) collective-permute-start(f32[10,256]{1,0:T(8,128)S(1)} %get-tuple-element.12), channel_id=1, source_target_pairs={{8,0},{16,8},{24,16},{32,24},{40,32},{48,40},{56,48},{64,56},{72,6... | collective-permute-start | bytes 30728 | tf_op jit(solution)/shard_map/ppermute | solution.py:25
  90.3 1.9 copy-start.1
  92.7 44.7 %collective-permute-start.2 = (f32[10,256]{1,0:T(8,128)S(1)}, f32[10,256]{1,0:T(8,128)S(1)}, u32[]{:S(2)}, u32[]{:S(2)}) collective-permute-start(f32[10,256]{1,0:T(8,128)S(1)} %get-tuple-element.9), channel_id=1, source_target_pairs={{0,8},{8,16},{16,24},{24,32},{32,40},{40,48},{48,56},{56,64},{64,7... | collective-permute-start | bytes 30728 | tf_op jit(solution)/shard_map/ppermute | solution.py:22
  94.6 42.8 %collective-permute-start.3 = (f32[10,256]{1,0:T(8,128)S(1)}, f32[10,256]{1,0:T(8,128)S(1)}, u32[]{:S(2)}, u32[]{:S(2)}) collective-permute-start(f32[10,256]{1,0:T(8,128)S(1)} %get-tuple-element.10), channel_id=1, source_target_pairs={{8,0},{16,8},{24,16},{32,24},{40,32},{48,40},{56,48},{64,56},{72,6... | collective-permute-start | bytes 30728 | tf_op jit(solution)/shard_map/ppermute | solution.py:25
  174.4 44.3 %collective-permute-start.4 = (f32[10,256]{1,0:T(8,128)S(1)}, f32[10,256]{1,0:T(8,128)S(1)}, u32[]{:S(2)}, u32[]{:S(2)}) collective-permute-start(f32[10,256]{1,0:T(8,128)S(1)} %get-tuple-element.6), channel_id=1, source_target_pairs={{0,8},{8,16},{16,24},{24,32},{32,40},{40,48},{48,56},{56,64},{64,7... | collective-permute-start | bytes 30728 | tf_op jit(solution)/shard_map/ppermute | solution.py:22
  176.3 42.3 %collective-permute-start.5 = (f32[10,256]{1,0:T(8,128)S(1)}, f32[10,256]{1,0:T(8,128)S(1)}, u32[]{:S(2)}, u32[]{:S(2)}) collective-permute-start(f32[10,256]{1,0:T(8,128)S(1)} %get-tuple-element.8), channel_id=1, source_target_pairs={{8,0},{16,8},{24,16},{32,24},{40,32},{48,40},{56,48},{64,56},{72,6... | collective-permute-start | bytes 30728 | tf_op jit(solution)/shard_map/ppermute | solution.py:25
  342.4 33.8 %copy-start.3 = (f32[20,256]{1,0:T(8,128)S(1)}, f32[20,256]{1,0:T(8,128)}, u32[]{:S(2)}) copy-start(f32[20,256]{1,0:T(8,128)} %reduce-scatter.2.cloned.1.call-done) | copy-start | bytes 61444
  343.2 11.2 %collective-permute-start.6 = (f32[20,256]{1,0:T(8,128)S(1)}, f32[20,256]{1,0:T(8,128)S(1)}, u32[]{:S(2)}, u32[]{:S(2)}) collective-permute-start(f32[20,256]{1,0:T(8,128)S(1)} %multiply_divide_fusion), channel_id=1, source_target_pairs={{0,1},{1,2},{2,3},{3,4},{4,5},{5,6},{6,7},{7,8},{8,9},{9,10},{10,1... | collective-permute-start | bytes 61448 | tf_op jit(solution)/shard_map/ppermute | solution.py:22
  347.5 8.2 %collective-permute-start.7 = (f32[20,256]{1,0:T(8,128)S(1)}, f32[20,256]{1,0:T(8,128)S(1)}, u32[]{:S(2)}, u32[]{:S(2)}) collective-permute-start(f32[20,256]{1,0:T(8,128)S(1)} %multiply_divide_fusion), channel_id=1, source_target_pairs={{1,0},{2,1},{3,2},{4,3},{5,4},{6,5},{7,6},{8,7},{9,8},{10,9},{11,1... | collective-permute-start | bytes 61448 | tf_op jit(solution)/shard_map/ppermute | solution.py:25
  360.2 11.2 %collective-permute-start.8 = (f32[20,256]{1,0:T(8,128)S(1)}, f32[20,256]{1,0:T(8,128)S(1)}, u32[]{:S(2)}, u32[]{:S(2)}) collective-permute-start(f32[20,256]{1,0:T(8,128)S(1)} %fusion.26), channel_id=1, source_target_pairs={{0,1},{1,2},{2,3},{3,4},{4,5},{5,6},{6,7},{7,8},{8,9},{9,10},{10,1... | collective-permute-start | bytes 61448 | tf_op jit(solution)/shard_map/ppermute | solution.py:22
  363.7 8.9 %collective-permute-start.9 = (f32[20,256]{1,0:T(8,128)S(1)}, f32[20,256]{1,0:T(8,128)S(1)}, u32[]{:S(2)}, u32[]{:S(2)}) collective-permute-start(f32[20,256]{1,0:T(8,128)S(1)} %fusion.26), channel_id=1, source_target_pairs={{1,0},{2,1},{3,2},{4,3},{5,4},{6,5},{7,6},{8,7},{9,8},{10,9},{11,1... | collective-permute-start | bytes 61448 | tf_op jit(solution)/shard_map/ppermute | solution.py:25
Sparse Core Ops, SparseCore 0:
  256.7 85.5 reduce-scatter.1
where the time goes:
time: 419 us
  blocking collectives  146 us (35%)
  local copies, waits for them, and re-layouts  93.9 us (22%)
  waiting for transfers between devices  88.2 us (21%)
  starting transfers between devices  45 us (11%)
  other arithmetic  27.3 us (7%)
  between operations  13.9 us (3%)
  matrix products  4.6 us (1%)
    all_gather x3, blocking collectives, derivative(): gathered = lax.all_gather(values, 'inst', axis=0, tiled=True)  111 us
    gather x5, local copies, waits for them, and re-layouts, neighbour_terms(): jnp.take(padded, flat_index, axis=1).reshape(padded.shape[0], NEIGH, cells)  89.2 us
    reduce_scatter x1, waiting for transfers between devices, per_device(): lax.psum_scatter(partial_terms, 'inst', scatter_dimension=1, tiled=True)  85.6 us
    all_gather x1, blocking collectives, per_device(): whole_correction = lax.all_gather(correction, 'inst', axis=1, tiled=True)  34.3 us
    ppermute x5, starting transfers between devices, padded_2(): lax.ppermute(lax.slice_in_dim(block, 0, width, axis=dim), axis, backward)  31.4 us
    select_n x5, other arithmetic, neighbour_terms(): jnp.take(padded, flat_index, axis=1).reshape(padded.shape[0], NEIGH, cells)  19.1 us
    ppermute x5, starting transfers between devices, padded_2(): lax.ppermute(lax.slice_in_dim(block, block.shape[dim] - width, None, axis...  13.6 us
  transfers between devices with their start and end apart: 11, of which 3 were waited for; matrix products, arithmetic and copies ran while one was open for 1% of the time, Pallas kernels for 0%

commit v1 on v0

--- a/solution.py
+++ b/solution.py
@@ -118,7 +118,9 @@
             - coarse_stencil(correction, share_index, share_weights)
         )
         correction = correction + RELAX * (coarse_rhs - applied) / share_diagonal
-    whole_correction = lax.all_gather(correction, "inst", axis=1, tiled=True)
+    whole_correction = jnp.concatenate(
+        lax.all_to_all(jnp.stack([correction] * lax.axis_size("inst")), "inst", 0, 0), axis=1
+    )
     return solution + jnp.dot(prolong_rows, whole_correction, precision=highest)
 
 

time: 419 us -> 402 us (0.959)
  the two profiles are of different devices: /device:TPU:128 before, /device:TPU:105 now
where the time goes in v1:
time: 402 us; the launch traced here: 401 us
  waiting for transfers between devices  98.5 us (25%)
  local copies, waits for them, and re-layouts  94.8 us (24%)
  blocking collectives  93.9 us (23%)
  starting transfers between devices  67.5 us (17%)
  other arithmetic  27.3 us (7%)
  between operations  13.9 us (3%)
  matrix products  4.59 us (1%)
    all_gather x3, blocking collectives, derivative(): gathered = lax.all_gather(values, 'inst', axis=0, tiled=True)  93.9 us
    reduce_scatter x1, waiting for transfers between devices, per_device(): lax.psum_scatter(partial_terms, 'inst', scatter_dimension=1, tiled=True)  90.2 us
    gather x5, local copies, waits for them, and re-layouts, neighbour_terms(): jnp.take(padded, flat_index, axis=1).reshape(padded.shape[0], NEIGH, cells)  89.3 us
    ppermute x5, starting transfers between devices, padded_2(): lax.ppermute(lax.slice_in_dim(block, block.shape[dim] - width, None, axis...  35.9 us
    select_n x5, other arithmetic, neighbour_terms(): jnp.take(padded, flat_index, axis=1).reshape(padded.shape[0], NEIGH, cells)  19.1 us
    ppermute x5, starting transfers between devices, padded_2(): lax.ppermute(lax.slice_in_dim(block, 0, width, axis=dim), axis, backward)  16.7 us
    all_to_all x1, starting transfers between devices, per_device(): lax.all_to_all(jnp.stack([correction] * lax.axis_size('inst')), 'inst', 0...  14.9 us
  transfers between devices with their start and end apart: 12, of which 4 were waited for; matrix products, arithmetic and copies ran while one was open for 1% of the time, Pallas kernels for 0%

profile of v1, /device:TPU:105, one launch (start us, length us, event | category | flops | bytes accessed | tf_op | source)
XLA Modules:
  0.0 400.5 jit_solution(65653028419003159)
XLA Ops:
  6.5 0.8 fusion.63
  7.3 5.2 %collective-permute-start = (f32[10,256]{1,0:T(8,128)S(1)}, f32[10,256]{1,0:T(8,128)S(1)}, u32[]{:S(2)}, u32[]{:S(2)}) collective-permute-start(f32[10,256]{1,0:T(8,128)S(1)} %get-tuple-element.11), channel_id=1, source_target_pairs={{0,8},{8,16},{16,24},{24,32},{32,40},{40,48},{48,56},{56,64},{64,7... | collective-permute-start | bytes 30728 | tf_op jit(solution)/shard_map/ppermute | solution.py:22
  12.5 1.9 collective-permute-start.1
  14.5 0.8 add_bitcast_fusion
  15.4 32.5 %all-gather = f32[8,10,2048]{2,1,0:T(8,128)S(1)} all-gather(f32[1,10,2048]{2,1,0:T(8,128)} %bitcast.51), channel_id=1, replica_groups=mesh['cell'=64,'inst'=8] {'inst'}, dimensions={0}, use_global_device_ids=true | all-gather | bytes 737280 | tf_op jit(solution)/shard_map/all_gather | solution.py:84
  48.2 0.7 add_bitcast_fusion.1
  49.0 0.3 mul.297
  49.7 0.4 copy.21
  50.1 27.9 %gather_fusion = f32[8192,10]{1,0:T(8,128)} fusion(f32[10,2560]{0,1:T(8,128)S(1)} %copy.21, s32[8192]{0:T(1024)S(1)} %fusion.27), kind=kCustom, calls=%fused_computation.clone | custom fusion | bytes 688128 | tf_op jit(solution)/shard_map/jit(_take)/gather | solution.py:56
  78.0 6.2 %broadcast_select_fusion.2 = f32[8192,10]{1,0:T(8,128)S(1)} fusion(f32[8192,10]{1,0:T(8,128)} %gather_fusion, pred[8192]{0:T(1024)(128)(4,1)S(1)} %compare_and_fusion), kind=kLoop, calls=%fused_computation.29 | loop fusion | flops 81920 | bytes 663552 | tf_op jit(solution)/shard_map/jit(_take)/select_n | solution.py:56
  84.2 1.6 multiply_reduce_fusion.2
  85.8 0.3 copy.22
  86.1 0.5 fusion.14
  86.6 11.2 %collective-permute-start.2 = (f32[10,256]{1,0:T(8,128)S(1)}, f32[10,256]{1,0:T(8,128)S(1)}, u32[]{:S(2)}, u32[]{:S(2)}) collective-permute-start(f32[10,256]{1,0:T(8,128)S(1)} %get-tuple-element.9), channel_id=1, source_target_pairs={{0,8},{8,16},{16,24},{24,32},{32,40},{40,48},{48,56},{56,64},{64,7... | collective-permute-start | bytes 30728 | tf_op jit(solution)/shard_map/ppermute | solution.py:22
  97.8 1.9 collective-permute-start.3
  99.7 31.5 %all-gather.1 = f32[8,10,2048]{2,1,0:T(8,128)S(1)} all-gather(f32[1,10,2048]{2,1,0:T(8,128)S(1)} %bitcast.48), channel_id=1, replica_groups=mesh['cell'=64,'inst'=8] {'inst'}, dimensions={0}, use_global_device_ids=true | all-gather | bytes 737280 | tf_op jit(solution)/shard_map/all_gather | solution.py:84
  131.4 0.4 copy.23
  131.8 27.9 %gather_fusion.1 = f32[8192,10]{1,0:T(8,128)} fusion(f32[10,2560]{0,1:T(8,128)S(1)} %copy.23, s32[8192]{0:T(1024)S(1)} %fusion.27), kind=kCustom, calls=%fused_computation.2.clone | custom fusion | bytes 688128 | tf_op jit(solution)/shard_map/jit(_take)/gather | solution.py:56
  159.7 6.2 %broadcast_select_fusion.1 = f32[8192,10]{1,0:T(8,128)S(1)} fusion(f32[8192,10]{1,0:T(8,128)} %gather_fusion.1, pred[8192]{0:T(1024)(128)(4,1)S(1)} %compare_and_fusion), kind=kLoop, calls=%fused_computation.28 | loop fusion | flops 81920 | bytes 663552 | tf_op jit(solution)/shard_map/jit(_take)/select_n | solution.py:56
  165.9 1.6 multiply_reduce_fusion.1
  167.5 0.3 copy.24
  167.8 0.5 fusion.8
  168.3 11.6 %collective-permute-start.4 = (f32[10,256]{1,0:T(8,128)S(1)}, f32[10,256]{1,0:T(8,128)S(1)}, u32[]{:S(2)}, u32[]{:S(2)}) collective-permute-start(f32[10,256]{1,0:T(8,128)S(1)} %get-tuple-element.6), channel_id=1, source_target_pairs={{0,8},{8,16},{16,24},{24,32},{32,40},{40,48},{48,56},{56,64},{64,7... | collective-permute-start | bytes 30728 | tf_op jit(solution)/shard_map/ppermute | solution.py:22
  179.8 1.9 collective-permute-start.5
  181.8 29.9 %all-gather.2 = f32[8,10,2048]{2,1,0:T(8,128)S(1)} all-gather(f32[1,10,2048]{2,1,0:T(8,128)S(1)} %bitcast.47), channel_id=1, replica_groups=mesh['cell'=64,'inst'=8] {'inst'}, dimensions={0}, use_global_device_ids=true | all-gather | bytes 737280 | tf_op jit(solution)/shard_map/all_gather | solution.py:84
  211.8 0.4 copy.26
  212.2 27.9 %gather_fusion.2 = f32[8192,10]{1,0:T(8,128)} fusion(f32[10,2560]{0,1:T(8,128)S(1)} %copy.26, s32[8192]{0:T(1024)S(1)} %fusion.27), kind=kCustom, calls=%fused_computation.3.clone | custom fusion | bytes 688128 | tf_op jit(solution)/shard_map/jit(_take)/gather | solution.py:56
  240.1 6.2 %broadcast_select_fusion = f32[8192,10]{1,0:T(8,128)S(1)} fusion(f32[8192,10]{1,0:T(8,128)} %gather_fusion.2, pred[8192]{0:T(1024)(128)(4,1)S(1)} %compare_and_fusion), kind=kLoop, calls=%fused_computation.27 | loop fusion | flops 81920 | bytes 663552 | tf_op jit(solution)/shard_map/jit(_take)/select_n | solution.py:56
  246.3 1.6 multiply_reduce_fusion
  247.9 0.3 copy.27
  248.2 0.4 fusion.2
  248.7 1.0 fusion.28
  249.9 90.2 %reduce-scatter.2.cloned.1.call-done = f32[20,256]{1,0:T(8,128)} async-done(((f32[20,2048]{1,0:T(8,128)}), f32[20,256]{1,0:T(8,128)}) %reduce-scatter.2.cloned.1.call-update) | async-done | bytes 20496 | tf_op jit(solution)/shard_map/reduce_scatter | solution.py:105
  340.1 0.8 multiply_divide_fusion
  340.9 3.8 collective-permute-start.6
  344.6 5.4 %collective-permute-start.7 = (f32[20,256]{1,0:T(8,128)S(1)}, f32[20,256]{1,0:T(8,128)S(1)}, u32[]{:S(2)}, u32[]{:S(2)}) collective-permute-start(f32[20,256]{1,0:T(8,128)S(1)} %multiply_divide_fusion), channel_id=1, source_target_pairs={{1,0},{2,1},{3,2},{4,3},{5,4},{6,5},{7,6},{8,7},{9,8},{10,9},{11,1... | collective-permute-start | bytes 61448 | tf_op jit(solution)/shard_map/ppermute | solution.py:25
  350.2 0.8 collective-permute-done.7
  351.2 2.8 gather_fusion.3
  354.2 0.2 multiply_reduce_fusion.4
  354.5 1.0 fusion.26
  355.5 4.2 %collective-permute-start.8 = (f32[20,256]{1,0:T(8,128)S(1)}, f32[20,256]{1,0:T(8,128)S(1)}, u32[]{:S(2)}, u32[]{:S(2)}) collective-permute-start(f32[20,256]{1,0:T(8,128)S(1)} %fusion.26), channel_id=1, source_target_pairs={{0,1},{1,2},{2,3},{3,4},{4,5},{5,6},{6,7},{7,8},{8,9},{9,10},{10,1... | collective-permute-start | bytes 61448 | tf_op jit(solution)/shard_map/ppermute | solution.py:22
  359.7 5.5 %collective-permute-start.9 = (f32[20,256]{1,0:T(8,128)S(1)}, f32[20,256]{1,0:T(8,128)S(1)}, u32[]{:S(2)}, u32[]{:S(2)}) collective-permute-start(f32[20,256]{1,0:T(8,128)S(1)} %fusion.26), channel_id=1, source_target_pairs={{1,0},{2,1},{3,2},{4,3},{5,4},{6,5},{7,6},{8,7},{9,8},{10,9},{11,1... | collective-permute-start | bytes 61448 | tf_op jit(solution)/shard_map/ppermute | solution.py:25
  365.5 0.7 collective-permute-done.9
  366.4 2.8 gather_fusion.4
  369.9 0.7 stack.2
  370.5 14.9 %all-to-all-start = ((f32[8,20,256]{2,1,0:T(8,128)}), f32[8,20,256]{2,1,0:T(8,128)S(1)}, u32[]{:S(2)}, u32[]{:S(2)}) async-start(f32[8,20,256]{2,1,0:T(8,128)} %stack.2), calls=%async_computation.1 | async-start | bytes 393216 | tf_op jit(solution)/shard_map/all_to_all | solution.py:122
  385.7 6.8 %all-to-all-done = f32[8,20,256]{2,1,0:T(8,128)S(1)} async-done(((f32[8,20,256]{2,1,0:T(8,128)}), f32[8,20,256]{2,1,0:T(8,128)S(1)}, u32[]{:S(2)}, u32[]{:S(2)}) %all-to-all-start) | async-done | bytes 163872 | tf_op jit(solution)/shard_map/all_to_all | solution.py:122
  392.6 1.1 convolution_add_fusion
  (66 shorter events, 3.1 us)
Async XLA Ops:
  6.5 43.1 %copy-start = (f32[10,2048]{1,0:T(8,128)S(1)}, f32[10,2048]{1,0:T(8,128)}, u32[]{:S(2)}) copy-start(f32[10,2048]{1,0:T(8,128)} %param.9) | copy-start | bytes 245764
  6.5 43.0 %copy-start.2 = (f32[4,2048]{1,0:T(4,128)S(1)}, f32[4,2048]{1,0:T(4,128)}, u32[]{:S(2)}) copy-start(f32[4,2048]{1,0:T(4,128)} %param.12) | copy-start | bytes 98308
  6.5 43.0 %copy-start.4 = (f32[2048]{0:T(1024)S(1)}, f32[2048]{0:T(1024)}, u32[]{:S(2)}) copy-start(f32[2048]{0:T(1024)} %param.13) | copy-start | bytes 24580
  6.5 333.5 %reduce-scatter.2.cloned.1.call-start = ((), (), s32[]{:S(2)}) async-start(), calls=%async_computation.2 | async-start | bytes 221184 | tf_op jit(solution)/shard_map/reduce_scatter | solution.py:105
  7.3 42.3 %collective-permute-start = (f32[10,256]{1,0:T(8,128)S(1)}, f32[10,256]{1,0:T(8,128)S(1)}, u32[]{:S(2)}, u32[]{:S(2)}) collective-permute-start(f32[10,256]{1,0:T(8,128)S(1)} %get-tuple-element.11), channel_id=1, source_target_pairs={{0,8},{8,16},{16,24},{24,32},{32,40},{40,48},{48,56},{56,64},{64,7... | collective-permute-start | bytes 30728 | tf_op jit(solution)/shard_map/ppermute | solution.py:22
  12.5 37.1 %collective-permute-start.1 = (f32[10,256]{1,0:T(8,128)S(1)}, f32[10,256]{1,0:T(8,128)S(1)}, u32[]{:S(2)}, u32[]{:S(2)}) collective-permute-start(f32[10,256]{1,0:T(8,128)S(1)} %get-tuple-element.12), channel_id=1, source_target_pairs={{8,0},{16,8},{24,16},{32,24},{40,32},{48,40},{56,48},{64,56},{72,6... | collective-permute-start | bytes 30728 | tf_op jit(solution)/shard_map/ppermute | solution.py:25
  84.2 1.9 copy-start.1
  86.6 44.7 %collective-permute-start.2 = (f32[10,256]{1,0:T(8,128)S(1)}, f32[10,256]{1,0:T(8,128)S(1)}, u32[]{:S(2)}, u32[]{:S(2)}) collective-permute-start(f32[10,256]{1,0:T(8,128)S(1)} %get-tuple-element.9), channel_id=1, source_target_pairs={{0,8},{8,16},{16,24},{24,32},{32,40},{40,48},{48,56},{56,64},{64,7... | collective-permute-start | bytes 30728 | tf_op jit(solution)/shard_map/ppermute | solution.py:22
  97.8 33.5 %collective-permute-start.3 = (f32[10,256]{1,0:T(8,128)S(1)}, f32[10,256]{1,0:T(8,128)S(1)}, u32[]{:S(2)}, u32[]{:S(2)}) collective-permute-start(f32[10,256]{1,0:T(8,128)S(1)} %get-tuple-element.10), channel_id=1, source_target_pairs={{8,0},{16,8},{24,16},{32,24},{40,32},{48,40},{56,48},{64,56},{72,6... | collective-permute-start | bytes 30728 | tf_op jit(solution)/shard_map/ppermute | solution.py:25
  168.3 43.4 %collective-permute-start.4 = (f32[10,256]{1,0:T(8,128)S(1)}, f32[10,256]{1,0:T(8,128)S(1)}, u32[]{:S(2)}, u32[]{:S(2)}) collective-permute-start(f32[10,256]{1,0:T(8,128)S(1)} %get-tuple-element.6), channel_id=1, source_target_pairs={{0,8},{8,16},{16,24},{24,32},{32,40},{40,48},{48,56},{56,64},{64,7... | collective-permute-start | bytes 30728 | tf_op jit(solution)/shard_map/ppermute | solution.py:22
  179.8 31.9 %collective-permute-start.5 = (f32[10,256]{1,0:T(8,128)S(1)}, f32[10,256]{1,0:T(8,128)S(1)}, u32[]{:S(2)}, u32[]{:S(2)}) collective-permute-start(f32[10,256]{1,0:T(8,128)S(1)} %get-tuple-element.8), channel_id=1, source_target_pairs={{8,0},{16,8},{24,16},{32,24},{40,32},{48,40},{56,48},{64,56},{72,6... | collective-permute-start | bytes 30728 | tf_op jit(solution)/shard_map/ppermute | solution.py:25
  340.1 29.6 %copy-start.3 = (f32[20,256]{1,0:T(8,128)S(1)}, f32[20,256]{1,0:T(8,128)}, u32[]{:S(2)}) copy-start(f32[20,256]{1,0:T(8,128)} %reduce-scatter.2.cloned.1.call-done) | copy-start | bytes 61444
  340.9 9.3 %collective-permute-start.6 = (f32[20,256]{1,0:T(8,128)S(1)}, f32[20,256]{1,0:T(8,128)S(1)}, u32[]{:S(2)}, u32[]{:S(2)}) collective-permute-start(f32[20,256]{1,0:T(8,128)S(1)} %multiply_divide_fusion), channel_id=1, source_target_pairs={{0,1},{1,2},{2,3},{3,4},{4,5},{5,6},{6,7},{7,8},{8,9},{9,10},{10,1... | collective-permute-start | bytes 61448 | tf_op jit(solution)/shard_map/ppermute | solution.py:22
  344.6 6.3 %collective-permute-start.7 = (f32[20,256]{1,0:T(8,128)S(1)}, f32[20,256]{1,0:T(8,128)S(1)}, u32[]{:S(2)}, u32[]{:S(2)}) collective-permute-start(f32[20,256]{1,0:T(8,128)S(1)} %multiply_divide_fusion), channel_id=1, source_target_pairs={{1,0},{2,1},{3,2},{4,3},{5,4},{6,5},{7,6},{8,7},{9,8},{10,9},{11,1... | collective-permute-start | bytes 61448 | tf_op jit(solution)/shard_map/ppermute | solution.py:25
  355.5 10.0 %collective-permute-start.8 = (f32[20,256]{1,0:T(8,128)S(1)}, f32[20,256]{1,0:T(8,128)S(1)}, u32[]{:S(2)}, u32[]{:S(2)}) collective-permute-start(f32[20,256]{1,0:T(8,128)S(1)} %fusion.26), channel_id=1, source_target_pairs={{0,1},{1,2},{2,3},{3,4},{4,5},{5,6},{6,7},{7,8},{8,9},{9,10},{10,1... | collective-permute-start | bytes 61448 | tf_op jit(solution)/shard_map/ppermute | solution.py:22
  359.7 6.4 %collective-permute-start.9 = (f32[20,256]{1,0:T(8,128)S(1)}, f32[20,256]{1,0:T(8,128)S(1)}, u32[]{:S(2)}, u32[]{:S(2)}) collective-permute-start(f32[20,256]{1,0:T(8,128)S(1)} %fusion.26), channel_id=1, source_target_pairs={{1,0},{2,1},{3,2},{4,3},{5,4},{6,5},{7,6},{8,7},{9,8},{10,9},{11,1... | collective-permute-start | bytes 61448 | tf_op jit(solution)/shard_map/ppermute | solution.py:25
  370.5 21.9 %all-to-all-start = ((f32[8,20,256]{2,1,0:T(8,128)}), f32[8,20,256]{2,1,0:T(8,128)S(1)}, u32[]{:S(2)}, u32[]{:S(2)}) async-start(f32[8,20,256]{2,1,0:T(8,128)} %stack.2), calls=%async_computation.1 | async-start | bytes 393216 | tf_op jit(solution)/shard_map/all_to_all | solution.py:122
Sparse Core Ops, SparseCore 0:
  249.9 90.1 reduce-scatter.1
